TPU v7x, 32 devices: a whole 2x2x4 slice. The times are simulated.
32 devices in a mesh: grp: 2 (over y), row: 8 (over z, x), col: 2 (over core).
Axes of the slice: x: 2, y: 2, z: 4, core: 2. Of those that a mesh axis runs over, the one named last changes fastest.
Arguments:
- queries: bfloat16 [8192, 2, 128], P(('grp', 'row', 'col')), parts along dimension 0, may hold values from -6 to 6
- keys: bfloat16 [8192, 2, 128], P(('grp', 'row', 'col')), parts along dimension 0, may hold values from -6 to 6
- values: bfloat16 [8192, 2, 128], P(('grp', 'row', 'col')), parts along dimension 0, may hold values from -6 to 6
Outputs:
- attended: bfloat16 [8192, 256], P(('grp', 'row', 'col')), parts along dimension 0
There are 2 independent parts, one for each index of `grp`. A program takes and returns all parts, laid end to end along the dimension named above; each array names one. Nothing has to cross between parts.
All inputs are finite; a program needn't handle non-finite values.
Results may differ from a plain program's by a relative error of at most 0.014.
Values may be sent and summed in bfloat16 or wider, within the bound.
A program may use at most 128 MiB of HBM per device.

v0:
```python
import math

import jax
import jax.numpy as jnp
from jax import lax
from jax.sharding import PartitionSpec as P


def joined(value, axis, join):
    pieces = jax.tree.map(lambda part: lax.all_gather(part, axis), value)
    head = jax.tree.map(lambda part: part[0], pieces)
    tail = jax.tree.map(lambda part: part[1:], pieces)
    total, _ = lax.scan(lambda total, share: (join(total, share), None), head, tail)
    return total


def attend(running, portion, offset, query_rows, widest=2048):
    key_rows, value_rows = portion
    length_rows = key_rows.shape[0]
    span_rows = math.gcd(length_rows, widest)
    scale = query_rows.shape[-1] ** (-0.5)
    key_blocks = key_rows.reshape(
        length_rows // span_rows, span_rows, key_rows.shape[1], key_rows.shape[2]
    )
    value_blocks = value_rows.reshape(
        length_rows // span_rows, span_rows, value_rows.shape[1], value_rows.shape[2]
    )

    def advance(carried, blocks):
        highest, summed, accum = carried
        key_block, value_block = blocks
        scores = (
            jnp.einsum("qhd,khd->hqk", query_rows, key_block, preferred_element_type=jnp.float32)
            * scale
        )
        raised = jnp.maximum(highest, jnp.max(scores, axis=-1))
        factor = jnp.exp(highest - raised)
        weights = jnp.exp(scores - raised[..., None]).astype(jnp.bfloat16)
        summed = summed * factor + jnp.sum(weights.astype(jnp.float32), axis=-1)
        accum = accum * factor[..., None] + jnp.einsum(
            "hqk,khd->hqd", weights, value_block, preferred_element_type=jnp.float32
        )
        return ((raised, summed, accum), None)

    running, _ = lax.scan(advance, running, (key_blocks, value_blocks))
    return running


def combine_parts(first, second):
    peak_one, total_one, accum_one = first
    peak_two, total_two, accum_two = second
    highest = jnp.maximum(peak_one, peak_two)
    factor_one = jnp.exp(peak_one - highest)
    factor_two = jnp.exp(peak_two - highest)
    summed = total_one * factor_one + total_two * factor_two
    accum = accum_one * factor_one[..., None] + accum_two * factor_two[..., None]
    return (highest, summed, accum)


def starting(heads, n_rows, width):
    return (
        jnp.full((heads, n_rows), -1e30, jnp.float32),
        jnp.zeros((heads, n_rows), jnp.float32),
        jnp.zeros((heads, n_rows, width), jnp.float32),
    )


def body(queries, keys, values):
    own_rows = queries.shape[0]
    heads = queries.shape[1]
    width = queries.shape[2]
    query_rows = lax.all_gather(queries, "col", axis=0, tiled=True)
    n_rows = query_rows.shape[0]
    folded = attend(
        starting(heads, n_rows, width),
        (
            lax.all_gather(keys, "row", axis=0, tiled=True),
            lax.all_gather(values, "row", axis=0, tiled=True),
        ),
        jnp.int32(0),
        query_rows=query_rows,
    )
    peak, summed, accum = folded
    peak, summed, accum = joined((peak, summed, accum), "col", combine_parts)
    offset = lax.axis_index("col") * own_rows
    summed = lax.dynamic_slice_in_dim(summed, offset, own_rows, 1)
    accum = lax.dynamic_slice_in_dim(accum, offset, own_rows, 1)
    result = accum / summed[..., None]
    output = jnp.transpose(result, (1, 0, 2)).reshape(own_rows, heads * width)
    return output.astype(jnp.bfloat16)


def solution(mesh):
    placed = (
        P(("grp", "row", "col"), None, None),
        P(("grp", "row", "col"), None, None),
        P(("grp", "row", "col"), None, None),
    )
    return jax.shard_map(
        body, mesh=mesh, in_specs=placed, out_specs=P(("grp", "row", "col"), None), check_vma=False
    )
```

profile of v0, /device:TPU:3, one launch (start us, length us, event | category | flops | bytes accessed | tf_op | source)
XLA Modules:
  0.0 115.8 jit_solution(9935838960127809299)
XLA Ops:
  6.5 0.0 all-gather.7.cloned.1.call-start
  6.5 1.6 %copy.13 = bf16[256,2,128]{2,0,1:T(8,128)(2,1)} copy(bf16[256,2,128]{2,1,0:T(2,128)(2,1)} %param.4) | data formatting | bytes 262144 | tf_op args[1]
  8.1 0.0 all-gather.7.cloned.1.call-update
  8.1 0.0 all-gather.9.cloned.1.call-start
  8.2 1.6 %copy.14 = bf16[256,2,128]{2,0,1:T(8,128)(2,1)} copy(bf16[256,2,128]{2,1,0:T(2,128)(2,1)} %param.5) | data formatting | bytes 262144 | tf_op args[2]
  9.7 0.0 all-gather.9.cloned.1.call-update
  9.8 0.0 all-gather.11.cloned.1.call-start
  9.8 0.9 copy.12
  10.8 2.3 %all_gather.23 = bf16[512,2,128]{2,0,1:T(8,128)(2,1)S(1)} all-gather(bf16[256,2,128]{2,0,1:T(8,128)(2,1)S(1)} %copy.12), channel_id=1, replica_groups=mesh['grp'=2,'row'=8,'col'=2] {'col'}, dimensions={0}, use_global_device_ids=true | all-gather | bytes 393216 | tf_op jit(solution)/shard_map/all_gather | solution.py:72
  13.1 35.6 %all-gather.7.cloned.1.call-done = bf16[2048,2,128]{2,0,1:T(8,128)(2,1)} async-done(((bf16[256,2,128]{2,0,1:T(8,128)(2,1)}), bf16[2048,2,128]{2,0,1:T(8,128)(2,1)}) %all-gather.7.cloned.1.call-update) | async-done | bytes 1048592 | tf_op jit(solution)/shard_map/all_gather | solution.py:77
  48.7 2.6 %multiply_reduce_fusion = (f32[2,512]{1,0:T(2,128)S(1)}, f32[2,512,2048]{2,1,0:T(8,128)S(1)}) fusion(bf16[512,2,128]{2,0,1:T(8,128)(2,1)S(1)} %all_gather.23, bf16[2048,2,128]{2,0,1:T(8,128)(2,1)} %all-gather.7.cloned.1.call-done), kind=kOutput, calls=%fused_computation.2 | convolution fusion | flops 541064192 | bytes 9703424 | tf_op jit(solution)/shard_map/while/body/eval_jaxpr/qhd,khd->hqk/dot_general | solution.py:33
  51.2 0.0 copy-start
  51.2 3.2 %copy-done = f32[2,512,2048]{2,1,0:T(8,128)} copy-done((f32[2,512,2048]{2,1,0:T(8,128)}, f32[2,512,2048]{2,1,0:T(8,128)S(1)}, u32[]{:S(2)}) %copy-start) | copy-done | bytes 8388632
  54.4 1.6 %convert_reduce_fusion = f32[2,512]{1,0:T(2,128)S(1)} fusion(f32[2,512]{1,0:T(2,128)S(1)} %broadcast_maximum_fusion, f32[2,512,2048]{2,1,0:T(8,128)S(1)} %get-tuple-element.60), kind=kLoop, calls=%fused_computation | loop fusion | flops 10484736 | bytes 8396800 | tf_op jit(solution)/shard_map/while/body/eval_jaxpr/reduce_sum | solution.py:39
  56.1 33.7 %all-gather.9.cloned.1.call-done = bf16[2048,2,128]{2,0,1:T(8,128)(2,1)} async-done(((bf16[256,2,128]{2,0,1:T(8,128)(2,1)}), bf16[2048,2,128]{2,0,1:T(8,128)(2,1)}) %all-gather.9.cloned.1.call-update) | async-done | bytes 1048592 | tf_op jit(solution)/shard_map/all_gather | solution.py:78
  89.8 6.0 %convolution_add_fusion = f32[2,512,128]{2,1,0:T(8,128)} fusion(bf16[2048,2,128]{2,0,1:T(8,128)(2,1)} %all-gather.9.cloned.1.call-done, f32[2,512,2048]{2,1,0:T(8,128)} %copy-done, f32[2,512]{1,0:T(2,128)S(1)} %broadcast_maximum_fusion, f32[2,512]{1,0:T(2,128)S(1)} %get-tuple-element.48), kind=kOutput, calls=%fused_computation.3 | convolution fusion | flops 543293440 | bytes 9969664 | tf_op jit(solution)/shard_map/while/body/eval_jaxpr/hqk,khd->hqd/dot_general | solution.py:40
  95.8 0.0 all-gather.11.cloned.1.call-update
  95.8 3.6 %all_gather.29 = f32[2,2,512]{2,1,0:T(2,128)S(1)} all-gather(f32[1,2,512]{2,1,0:T(2,128)S(1)} %get-tuple-element.47), channel_id=1, replica_groups=mesh['grp'=2,'row'=8,'col'=2] {'col'}, dimensions={0}, use_global_device_ids=true | all-gather | bytes 12288 | tf_op jit(solution)/shard_map/all_gather | solution.py:10
  99.4 1.8 %all-gather.2 = f32[2,2,512]{2,1,0:T(2,128)S(1)} all-gather(f32[1,2,512]{2,1,0:T(2,128)S(1)} %get-tuple-element.56), channel_id=3, replica_groups=mesh['grp'=2,'row'=8,'col'=2] {'col'}, dimensions={0}, use_global_device_ids=true | all-gather | bytes 12288 | tf_op jit(solution)/shard_map/all_gather | solution.py:10
  101.3 5.6 %all-gather.11.cloned.1.call-done = f32[4,512,128]{2,1,0:T(8,128)} async-done(((f32[2,512,128]{2,1,0:T(8,128)}), f32[4,512,128]{2,1,0:T(8,128)}) %all-gather.11.cloned.1.call-update) | async-done | bytes 1048592 | tf_op jit(solution)/shard_map/all_gather | solution.py:10
  106.8 1.3 %fusion.5 = (f32[2,512,128]{2,1,0:T(8,128)S(1)}, f32[2,512,128]{2,1,0:T(8,128)S(1)}) fusion(f32[4,512,128]{2,1,0:T(8,128)} %all-gather.11.cloned.1.call-done), kind=kLoop, calls=%fused_computation.25 | loop fusion | bytes 2097152 | tf_op jit(solution)/shard_map/slice | solution.py:11
  108.2 0.1 copy.20
  108.3 0.1 copy.21
  108.5 0.8 copy.17
  (7 shorter events, 0.1 us)
Async XLA Ops:
  6.5 42.1 %all-gather.7.cloned.1.call-start = ((), (), s32[]{:S(2)}) async-start(), calls=%async_computation | async-start | bytes 1179648 | tf_op jit(solution)/shard_map/all_gather | solution.py:77
  8.1 81.7 %all-gather.9.cloned.1.call-start = ((), (), s32[]{:S(2)}) async-start(), calls=%async_computation.1 | async-start | bytes 1179648 | tf_op jit(solution)/shard_map/all_gather | solution.py:78
  9.8 97.1 %all-gather.11.cloned.1.call-start = ((), (), s32[]{:S(2)}) async-start(), calls=%async_computation.2 | async-start | bytes 1572864 | tf_op jit(solution)/shard_map/all_gather | solution.py:10
  51.2 3.2 %copy-start = (f32[2,512,2048]{2,1,0:T(8,128)}, f32[2,512,2048]{2,1,0:T(8,128)S(1)}, u32[]{:S(2)}) copy-start(f32[2,512,2048]{2,1,0:T(8,128)S(1)} %get-tuple-element.60) | copy-start | bytes 25165828
Sparse Core Ops, SparseCore 0:
  9.5 39.0 all-gather.6
  50.8 38.9 all-gather.8
  96.0 10.8 all-gather.10
where the time goes:
time: 117 us; the launch traced here: 116 us
  waiting for transfers between devices  75 us (64%)
  between operations  13.2 us (11%)
  local copies, waits for them, and re-layouts  9.6 us (8%)
  matrix products  8.54 us (7%)
  blocking collectives  7.68 us (7%)
  other arithmetic  1.72 us (1%)
    all_gather x1, waiting for transfers between devices, body(): lax.all_gather(keys, 'row', axis=0, tiled=True)  35.6 us
    all_gather x1, waiting for transfers between devices, body(): lax.all_gather(values, 'row', axis=0, tiled=True)  33.7 us
    unnamed x7, local copies, waits for them, and re-layouts  7.52 us
    dot_general x1, matrix products, advance(): jnp.einsum('hqk,khd->hqd', weights, value_block, preferred_element_type=j...  5.98 us
    all_gather x1, waiting for transfers between devices, joined(): pieces = jax.tree.map(lambda part: lax.all_gather(part, axis), value)  5.58 us
    all_gather x2, blocking collectives, joined(): pieces = jax.tree.map(lambda part: lax.all_gather(part, axis), value)  5.37 us
    dot_general x1, matrix products, advance(): jnp.einsum('qhd,khd->hqk', query_rows, key_block, preferred_element_type=...  2.55 us
  transfers between devices with their start and end apart: 3, of which 3 were waited for; matrix products, arithmetic and copies ran while one was open for 6% of the time, Pallas kernels for 0%

commit v1 on v0

v1 whole, which is shorter than its diff:
```python
import functools
import math

import jax
import jax.numpy as jnp
from jax import lax
from jax.experimental import pallas as pl
from jax.experimental.pallas import tpu as pltpu
from jax.sharding import PartitionSpec as P

MESH = pl.DeviceIdType.MESH


def kernel(
    rows, cores, q_ref, k_ref, v_ref, o_ref,
    stage, kv, qs, part, stat, got, got_stat, peak, total, accum,
    own_send, own_recv, pair_send, fwd_send, kv_recv, q_send, q_recv,
    out_send, out_recv, stat_send, stat_recv,
):
    tokens, heads, width = q_ref.shape
    group = rows // 2
    bits = [1 << n for n in range(group.bit_length() - 1)]
    span = cores * tokens
    rate = width ** -0.5 * math.log2(math.e)

    r = lax.axis_index("row")
    c = lax.axis_index("col")
    sib = lax.rem(c + 1, cores)
    far = lax.rem(r + group, rows)

    def across(bit):
        return r + bit * (1 - 2 * lax.rem(r // bit, 2))

    def at(row, core):
        return {"row": row, "col": core}

    barrier = pltpu.get_barrier_semaphore()
    pl.semaphore_signal(barrier, inc=1, device_id=at(r, sib), device_id_type=MESH)
    for row in [across(bit) for bit in bits] + [far]:
        for h in range(cores):
            pl.semaphore_signal(barrier, inc=1, device_id=at(row, h), device_id_type=MESH)

    for h in range(heads):
        stage[h, 0] = k_ref[:, h, :]
        stage[h, 1] = v_ref[:, h, :]
        stage[h, 2] = q_ref[:, h, :]
    pl.semaphore_wait(barrier, 1 + cores * (len(bits) + 1))

    def remote(src, dst, send, recv, row, core):
        return pltpu.make_async_remote_copy(
            src_ref=src, dst_ref=dst, send_sem=send, recv_sem=recv,
            device_id=at(row, core), device_id_type=MESH,
        )

    sends = []

    def go(copy):
        copy.start()
        sends.append(copy)

    kv_sib = remote(stage.at[sib, pl.ds(0, 2)], kv.at[0, c], own_send.at[0], own_recv.at[0], r, sib)
    q_sib = remote(stage.at[sib, 2], qs.at[0, c], own_send.at[1], own_recv.at[1], r, sib)
    go(kv_sib)
    go(q_sib)
    for n in reversed(range(len(bits))):
        for h in range(cores):
            go(remote(
                stage.at[h, pl.ds(0, 2)], kv.at[bits[n], c], pair_send.at[n, h],
                kv_recv.at[bits[n], c], across(bits[n]), h,
            ))
    for h in range(cores):
        go(remote(stage.at[h, 2], qs.at[1, c], q_send.at[h], q_recv.at[c], far, h))

    kv[0, c] = stage[c, 0:2]
    qs[0, c] = stage[c, 2]

    peak[...] = jnp.full_like(peak, -1e30)
    total[...] = jnp.zeros_like(total)
    accum[...] = jnp.zeros_like(accum)

    def tile(i, j):
        q = qs[i].reshape(span, width)
        k = kv[j, :, 0].reshape(span, width)
        v = kv[j, :, 1].reshape(span, width)
        s = lax.dot_general(q, k, (((1,), (1,)), ((), ())), preferred_element_type=jnp.float32)
        before = peak[i]
        now = jnp.maximum(before, jnp.max(s, axis=-1, keepdims=True))
        fade = jnp.exp2((before - now) * rate)
        w = jnp.exp2((s - now) * rate).astype(jnp.bfloat16)
        peak[i] = now
        total[i] = total[i] * fade + jnp.sum(w.astype(jnp.float32), axis=-1, keepdims=True)
        accum[i] = accum[i] * fade + jnp.dot(w, v, preferred_element_type=jnp.float32)

    def tiles(i, low, high):
        if high - low == 1:
            tile(i, low)
        else:
            pl.loop(low, high)(lambda j: tile(i, j))

    def finish(i):
        done = accum[i] / total[i]
        level = peak[i] * rate + jnp.log2(total[i])
        flat = jnp.broadcast_to(level, (span, 128)).T[0:8]
        return done.astype(jnp.bfloat16), flat

    def arrived(j):
        for s in range(cores):
            remote(stage.at[0, pl.ds(0, 2)], kv.at[j, s], own_send.at[0], kv_recv.at[j, s], r, sib).wait_recv()
            for n, bit in enumerate(bits):
                if j % (2 * bit) == 0:
                    go(remote(
                        kv.at[j, s], kv.at[j + bit, s], fwd_send.at[j, n, s],
                        kv_recv.at[j + bit, s], across(bit), c,
                    ))

    kv_sib.wait_recv()
    q_sib.wait_recv()
    tiles(0, 0, 1)
    order = sorted(range(1, group), key=lambda j: (bin(j).count("1"), -j))
    for j in order[:-1]:
        arrived(j)
    tiles(0, 1, group - 1)
    for s in range(cores):
        remote(stage.at[0, 2], qs.at[1, s], q_send.at[0], q_recv.at[s], r, sib).wait_recv()
    tiles(1, 0, group - 1)
    arrived(order[-1])
    tiles(1, group - 1, group)

    done, flat = finish(1)
    for s in range(cores):
        part[1, s] = done[s * tokens:(s + 1) * tokens]
        stat[1, s] = flat[:, s * tokens:(s + 1) * tokens]
        go(remote(stat.at[1, s], got_stat.at[1, c], stat_send.at[1, s], stat_recv.at[1, c], far, s))
        go(remote(part.at[1, s], got.at[1, c], out_send.at[1, s], out_recv.at[1, c], far, s))

    tiles(0, group - 1, group)
    done, flat = finish(0)
    for s in range(cores):
        part[0, s] = done[s * tokens:(s + 1) * tokens]
        stat[0, s] = flat[:, s * tokens:(s + 1) * tokens]
    stat_sib = remote(stat.at[0, sib], got_stat.at[0, c], stat_send.at[0, 0], stat_recv.at[0, 0], r, sib)
    out_sib = remote(part.at[0, sib], got.at[0, c], out_send.at[0, 0], out_recv.at[0, 0], r, sib)
    go(stat_sib)
    go(out_sib)
    got[0, c] = part[0, c]
    got_stat[0, c] = stat[0, c]
    stat_sib.wait_recv()
    out_sib.wait_recv()
    for h in range(cores):
        remote(stat.at[1, 0], got_stat.at[1, h], stat_send.at[1, 0], stat_recv.at[1, h], r, sib).wait_recv()
        remote(part.at[1, 0], got.at[1, h], out_send.at[1, 0], out_recv.at[1, h], r, sib).wait_recv()
    for h in range(heads):
        one, two = got_stat[0, h], got_stat[1, h]
        top = jnp.maximum(one, two)
        one, two = jnp.exp2(one - top), jnp.exp2(two - top)
        share = one / (one + two)
        share = jnp.broadcast_to(share[0:1], (128, tokens)).T
        near, away = got[0, h].astype(jnp.float32), got[1, h].astype(jnp.float32)
        o_ref[:, h * width:(h + 1) * width] = (away + (near - away) * share).astype(o_ref.dtype)
    for copy in sends:
        copy.wait_send()


def solution(mesh):
    rows, cores = mesh.shape["row"], mesh.shape["col"]
    group = rows // 2
    levels = group.bit_length() - 1

    def body(queries, keys, values):
        tokens, heads, width = queries.shape
        span = cores * tokens
        dma = pltpu.SemaphoreType.DMA
        bf16, f32 = jnp.bfloat16, jnp.float32
        return pl.pallas_call(
            functools.partial(kernel, rows, cores),
            out_shape=jax.ShapeDtypeStruct((tokens, heads * width), bf16),
            in_specs=[pl.BlockSpec(memory_space=pltpu.VMEM)] * 3,
            out_specs=pl.BlockSpec(memory_space=pltpu.VMEM),
            scratch_shapes=[
                pltpu.VMEM((heads, 3, tokens, width), bf16),
                pltpu.VMEM((group, cores, 2, tokens, width), bf16),
                pltpu.VMEM((2, cores, tokens, width), bf16),
                pltpu.VMEM((2, cores, tokens, width), bf16),
                pltpu.VMEM((2, cores, 8, tokens), f32),
                pltpu.VMEM((2, heads, tokens, width), bf16),
                pltpu.VMEM((2, heads, 8, tokens), f32),
                pltpu.VMEM((2, span, 1), f32),
                pltpu.VMEM((2, span, 1), f32),
                pltpu.VMEM((2, span, width), f32),
                dma((2,)), dma((2,)), dma((levels, cores)), dma((group, levels, cores)),
                dma((group, cores)), dma((cores,)), dma((cores,)),
                dma((2, cores)), dma((2, cores)), dma((2, cores)), dma((2, cores)),
            ],
            compiler_params=pltpu.CompilerParams(
                collective_id=0, has_side_effects=True, vmem_limit_bytes=48 * 1024 * 1024
            ),
        )(queries, keys, values)

    spec = P(("grp", "row", "col"), None, None)
    return jax.shard_map(
        body, mesh=mesh, in_specs=(spec,) * 3,
        out_specs=P(("grp", "row", "col"), None), check_vma=False,
    )
```

time: 117 us -> 32.3 us (0.28)
  the two profiles are of different devices: /device:TPU:3 before, /device:TPU:1 now
where the time goes in v1:
time: 32.3 us; the launch traced here: 32.2 us
  Pallas kernels  28.8 us (89%)
  local copies, waits for them, and re-layouts  3.37 us (10%)
    pallas_call x1, Pallas kernels, body(): pl.pallas_call(functools.partial(kernel, rows, cores), out_shape=jax.Shap...  28.8 us
    unnamed x7, local copies, waits for them, and re-layouts  3.37 us

profile of v1, /device:TPU:1, one launch (start us, length us, event | category | flops | bytes accessed | tf_op | source)
XLA Modules:
  0.0 32.2 jit_solution(10677729862207734137)
XLA Ops:
  0.0 0.0 copy-start
  0.0 0.9 %copy-done = bf16[256,2,128]{2,1,0:T(2,128)(2,1)S(1)} copy-done((bf16[256,2,128]{2,1,0:T(2,128)(2,1)S(1)}, bf16[256,2,128]{2,1,0:T(2,128)(2,1)}, u32[]{:S(2)}) %copy-start) | copy-done | bytes 131096
  0.9 0.0 copy-start.1
  0.9 0.9 %copy-done.1 = bf16[256,2,128]{2,1,0:T(2,128)(2,1)S(1)} copy-done((bf16[256,2,128]{2,1,0:T(2,128)(2,1)S(1)}, bf16[256,2,128]{2,1,0:T(2,128)(2,1)}, u32[]{:S(2)}) %copy-start.1) | copy-done | bytes 131096
  1.8 0.0 copy-start.2
  1.8 0.9 %copy-done.2 = bf16[256,2,128]{2,1,0:T(2,128)(2,1)S(1)} copy-done((bf16[256,2,128]{2,1,0:T(2,128)(2,1)S(1)}, bf16[256,2,128]{2,1,0:T(2,128)(2,1)}, u32[]{:S(2)}) %copy-start.2) | copy-done | bytes 131096
  2.7 28.8 %shard_map.37 = bf16[256,256]{1,0:T(8,128)(2,1)S(1)} custom-call(bf16[256,2,128]{2,1,0:T(2,128)(2,1)S(1)} %copy-done, bf16[256,2,128]{2,1,0:T(2,128)(2,1)S(1)} %copy-done.1, bf16[256,2,128]{2,1,0:T(2,128)(2,1)S(1)} %copy-done.2), custom_call_target="tpu_custom_call" | custom-call | tf_op jit(solution)/shard_map/pallas_call | solution.py:174
  31.5 0.7 %copy.5 = bf16[256,256]{1,0:T(8,128)(2,1)} copy(bf16[256,256]{1,0:T(8,128)(2,1)S(1)} %shard_map.37) | data formatting | bytes 262144
Async XLA Ops:
  0.0 0.9 %copy-start = (bf16[256,2,128]{2,1,0:T(2,128)(2,1)S(1)}, bf16[256,2,128]{2,1,0:T(2,128)(2,1)}, u32[]{:S(2)}) copy-start(bf16[256,2,128]{2,1,0:T(2,128)(2,1)} %q_ref.1) | copy-start | bytes 393220
  0.9 0.9 %copy-start.1 = (bf16[256,2,128]{2,1,0:T(2,128)(2,1)S(1)}, bf16[256,2,128]{2,1,0:T(2,128)(2,1)}, u32[]{:S(2)}) copy-start(bf16[256,2,128]{2,1,0:T(2,128)(2,1)} %k_ref.1) | copy-start | bytes 393220
  1.8 0.9 %copy-start.2 = (bf16[256,2,128]{2,1,0:T(2,128)(2,1)S(1)}, bf16[256,2,128]{2,1,0:T(2,128)(2,1)}, u32[]{:S(2)}) copy-start(bf16[256,2,128]{2,1,0:T(2,128)(2,1)} %v_ref.1) | copy-start | bytes 393220

commit v2 on v1

--- a/solution.py
+++ b/solution.py
@@ -12,16 +12,23 @@
 
 
 def kernel(
-    rows, cores, q_ref, k_ref, v_ref, o_ref,
-    stage, kv, qs, part, stat, got, got_stat, peak, total, accum,
-    own_send, own_recv, pair_send, fwd_send, kv_recv, q_send, q_recv,
+    rows, cores, q_hbm, k_hbm, v_hbm, o_ref,
+    raw, stage, kv, qs, part, stat, got, got_stat, peak, total, accum,
+    load, own_send, own_recv, pair_send, fwd_send, kv_recv, q_send, q_recv,
     out_send, out_recv, stat_send, stat_recv,
 ):
-    tokens, heads, width = q_ref.shape
+    tokens, heads, width = q_hbm.shape
     group = rows // 2
     bits = [1 << n for n in range(group.bit_length() - 1)]
     span = cores * tokens
     rate = width ** -0.5 * math.log2(math.e)
+
+    loads = [
+        pltpu.make_async_copy(ref, raw.at[n], load.at[n])
+        for n, ref in enumerate((k_hbm, v_hbm, q_hbm))
+    ]
+    for copy in loads:
+        copy.start()
 
     r = lax.axis_index("row")
     c = lax.axis_index("col")
@@ -40,10 +47,10 @@
         for h in range(cores):
             pl.semaphore_signal(barrier, inc=1, device_id=at(row, h), device_id_type=MESH)
 
-    for h in range(heads):
-        stage[h, 0] = k_ref[:, h, :]
-        stage[h, 1] = v_ref[:, h, :]
-        stage[h, 2] = q_ref[:, h, :]
+    for n, copy in enumerate(loads):
+        copy.wait()
+        for h in range(heads):
+            stage[h, n] = raw[n, :, h, :]
     pl.semaphore_wait(barrier, 1 + cores * (len(bits) + 1))
 
     def remote(src, dst, send, recv, row, core):
@@ -78,30 +85,34 @@
     total[...] = jnp.zeros_like(total)
     accum[...] = jnp.zeros_like(accum)
 
-    def tile(i, j):
-        q = qs[i].reshape(span, width)
+    def tile(i, s, j):
         k = kv[j, :, 0].reshape(span, width)
         v = kv[j, :, 1].reshape(span, width)
-        s = lax.dot_general(q, k, (((1,), (1,)), ((), ())), preferred_element_type=jnp.float32)
-        before = peak[i]
-        now = jnp.maximum(before, jnp.max(s, axis=-1, keepdims=True))
+        scores = lax.dot_general(
+            qs[i, s], k, (((1,), (1,)), ((), ())), preferred_element_type=jnp.float32
+        )
+        before = peak[i, s]
+        now = jnp.maximum(before, jnp.max(scores, axis=-1, keepdims=True))
         fade = jnp.exp2((before - now) * rate)
-        w = jnp.exp2((s - now) * rate).astype(jnp.bfloat16)
-        peak[i] = now
-        total[i] = total[i] * fade + jnp.sum(w.astype(jnp.float32), axis=-1, keepdims=True)
-        accum[i] = accum[i] * fade + jnp.dot(w, v, preferred_element_type=jnp.float32)
-
-    def tiles(i, low, high):
+        w = jnp.exp2((scores - now) * rate).astype(jnp.bfloat16)
+        peak[i, s] = now
+        total[i, s] = total[i, s] * fade + jnp.sum(w.astype(jnp.float32), axis=-1, keepdims=True)
+        accum[i, s] = accum[i, s] * fade + jnp.dot(w, v, preferred_element_type=jnp.float32)
+
+    def tiles(i, low, high, parts=range(cores)):
+        def step(j):
+            for s in parts:
+                tile(i, s, j)
+
         if high - low == 1:
-            tile(i, low)
+            step(low)
         else:
-            pl.loop(low, high)(lambda j: tile(i, j))
-
-    def finish(i):
-        done = accum[i] / total[i]
-        level = peak[i] * rate + jnp.log2(total[i])
-        flat = jnp.broadcast_to(level, (span, 128)).T[0:8]
-        return done.astype(jnp.bfloat16), flat
+            pl.loop(low, high)(step)
+
+    def finish(i, s):
+        part[i, s] = (accum[i, s] / total[i, s]).astype(jnp.bfloat16)
+        level = peak[i, s] * rate + jnp.log2(total[i, s])
+        stat[i, s] = jnp.broadcast_to(level, (tokens, 128)).T[0:8]
 
     def arrived(j):
         for s in range(cores):
@@ -124,20 +135,15 @@
         remote(stage.at[0, 2], qs.at[1, s], q_send.at[0], q_recv.at[s], r, sib).wait_recv()
     tiles(1, 0, group - 1)
     arrived(order[-1])
-    tiles(1, group - 1, group)
-
-    done, flat = finish(1)
     for s in range(cores):
-        part[1, s] = done[s * tokens:(s + 1) * tokens]
-        stat[1, s] = flat[:, s * tokens:(s + 1) * tokens]
+        tiles(1, group - 1, group, (s,))
+        finish(1, s)
         go(remote(stat.at[1, s], got_stat.at[1, c], stat_send.at[1, s], stat_recv.at[1, c], far, s))
         go(remote(part.at[1, s], got.at[1, c], out_send.at[1, s], out_recv.at[1, c], far, s))
 
     tiles(0, group - 1, group)
-    done, flat = finish(0)
     for s in range(cores):
-        part[0, s] = done[s * tokens:(s + 1) * tokens]
-        stat[0, s] = flat[:, s * tokens:(s + 1) * tokens]
+        finish(0, s)
     stat_sib = remote(stat.at[0, sib], got_stat.at[0, c], stat_send.at[0, 0], stat_recv.at[0, 0], r, sib)
     out_sib = remote(part.at[0, sib], got.at[0, c], out_send.at[0, 0], out_recv.at[0, 0], r, sib)
     go(stat_sib)
@@ -168,15 +174,15 @@
 
     def body(queries, keys, values):
         tokens, heads, width = queries.shape
-        span = cores * tokens
         dma = pltpu.SemaphoreType.DMA
         bf16, f32 = jnp.bfloat16, jnp.float32
         return pl.pallas_call(
             functools.partial(kernel, rows, cores),
             out_shape=jax.ShapeDtypeStruct((tokens, heads * width), bf16),
-            in_specs=[pl.BlockSpec(memory_space=pltpu.VMEM)] * 3,
+            in_specs=[pl.BlockSpec(memory_space=pltpu.HBM)] * 3,
             out_specs=pl.BlockSpec(memory_space=pltpu.VMEM),
             scratch_shapes=[
+                pltpu.VMEM((3, tokens, heads, width), bf16),
                 pltpu.VMEM((heads, 3, tokens, width), bf16),
                 pltpu.VMEM((group, cores, 2, tokens, width), bf16),
                 pltpu.VMEM((2, cores, tokens, width), bf16),
@@ -184,15 +190,15 @@
                 pltpu.VMEM((2, cores, 8, tokens), f32),
                 pltpu.VMEM((2, heads, tokens, width), bf16),
                 pltpu.VMEM((2, heads, 8, tokens), f32),
-                pltpu.VMEM((2, span, 1), f32),
-                pltpu.VMEM((2, span, 1), f32),
-                pltpu.VMEM((2, span, width), f32),
-                dma((2,)), dma((2,)), dma((levels, cores)), dma((group, levels, cores)),
+                pltpu.VMEM((2, cores, tokens, 1), f32),
+                pltpu.VMEM((2, cores, tokens, 1), f32),
+                pltpu.VMEM((2, cores, tokens, width), f32),
+                dma((3,)), dma((2,)), dma((2,)), dma((levels, cores)), dma((group, levels, cores)),
                 dma((group, cores)), dma((cores,)), dma((cores,)),
                 dma((2, cores)), dma((2, cores)), dma((2, cores)), dma((2, cores)),
             ],
             compiler_params=pltpu.CompilerParams(
-                collective_id=0, has_side_effects=True, vmem_limit_bytes=48 * 1024 * 1024
+                collective_id=0, has_side_effects=True, vmem_limit_bytes=63 * 1024 * 1024
             ),
         )(queries, keys, values)
 

time: 32.3 us -> 28.5 us (0.88)
  the two profiles are of different devices: /device:TPU:1 before, /device:TPU:3 now
where the time goes in v2:
time: 28.5 us; the launch traced here: 28.4 us
  Pallas kernels  26.8 us (94%)
  local copies, waits for them, and re-layouts  1.57 us (6%)
    pallas_call x1, Pallas kernels, body(): pl.pallas_call(functools.partial(kernel, rows, cores), out_shape=jax.Shap...  26.8 us
    unnamed x1, local copies, waits for them, and re-layouts  1.57 us

profile of v2, /device:TPU:3, one launch (start us, length us, event | category | flops | bytes accessed | tf_op | source)
XLA Modules:
  0.0 28.4 jit_solution(16277953555590385755)
XLA Ops:
  0.0 26.8 %shard_map.37 = bf16[256,256]{1,0:T(8,128)(2,1)} custom-call(bf16[256,2,128]{2,1,0:T(2,128)(2,1)} %q_hbm.1, bf16[256,2,128]{2,1,0:T(2,128)(2,1)} %k_hbm.1, bf16[256,2,128]{2,1,0:T(2,128)(2,1)} %v_hbm.1), custom_call_target="tpu_custom_call" | custom-call | tf_op jit(solution)/shard_map/pallas_call | solution.py:179
  26.8 1.6 %copy.5 = bf16[256,256]{1,0:T(8,128)(2,1)} copy(bf16[256,256]{1,0:T(8,128)(2,1)} %shard_map.37) | data formatting | bytes 262144

commit v3 on v2

--- a/solution.py
+++ b/solution.py
@@ -198,9 +198,9 @@
                 dma((2, cores)), dma((2, cores)), dma((2, cores)), dma((2, cores)),
             ],
             compiler_params=pltpu.CompilerParams(
-                collective_id=0, has_side_effects=True, vmem_limit_bytes=63 * 1024 * 1024
+                collective_id=0, has_side_effects=True, vmem_limit_bytes=48 * 1024 * 1024
             ),
-        )(queries, keys, values)
+        )(*[pltpu.with_memory_space_constraint(x, pltpu.HBM) for x in (queries, keys, values)])
 
     spec = P(("grp", "row", "col"), None, None)
     return jax.shard_map(

time: 28.5 us -> 27 us (0.947)
  local copies, waits for them, and re-layouts: 1.57 us -> 0.66 us
  Pallas kernels: 26.8 us -> 26.2 us
    unnamed x1, local copies, waits for them, and re-layouts: 1.57 us -> 0.66 us
    pallas_call x1, Pallas kernels: 26.8 us -> 26.2 us  [body(): pl.pallas_call(functools.partial(kernel, rows, cores), out_shape=jax.Shap...]
where the time goes in v3:
time: 27 us; the launch traced here: 26.9 us
  Pallas kernels  26.2 us (97%)
  local copies, waits for them, and re-layouts  0.66 us (2%)
    pallas_call x1, Pallas kernels, body(): pl.pallas_call(functools.partial(kernel, rows, cores), out_shape=jax.Shap...  26.2 us
    unnamed x1, local copies, waits for them, and re-layouts  0.66 us

profile of v3, /device:TPU:3, one launch (start us, length us, event | category | flops | bytes accessed | tf_op | source)
XLA Modules:
  0.0 26.9 jit_solution(127096897244359064)
XLA Ops:
  0.0 26.2 %shard_map.37 = bf16[256,256]{1,0:T(8,128)(2,1)S(1)} custom-call(bf16[256,2,128]{2,1,0:T(2,128)(2,1)} %q_hbm.1, bf16[256,2,128]{2,1,0:T(2,128)(2,1)} %k_hbm.1, bf16[256,2,128]{2,1,0:T(2,128)(2,1)} %v_hbm.1), custom_call_target="tpu_custom_call" | custom-call | tf_op jit(solution)/shard_map/pallas_call | solution.py:179
  26.2 0.7 %copy.5 = bf16[256,256]{1,0:T(8,128)(2,1)} copy(bf16[256,256]{1,0:T(8,128)(2,1)S(1)} %shard_map.37) | data formatting | bytes 262144

commit v4 on v3

--- a/solution.py
+++ b/solution.py
@@ -104,8 +104,9 @@
             for s in parts:
                 tile(i, s, j)
 
-        if high - low == 1:
-            step(low)
+        if high - low <= 4:
+            for j in range(low, high):
+                step(j)
         else:
             pl.loop(low, high)(step)
 

time: 27 us -> 26.5 us (0.981)
  the two profiles are of different devices: /device:TPU:3 before, /device:TPU:9 now
where the time goes in v4:
time: 26.5 us; the launch traced here: 26.4 us
  Pallas kernels  25.7 us (97%)
  local copies, waits for them, and re-layouts  0.66 us (2%)
    pallas_call x1, Pallas kernels, body(): pl.pallas_call(functools.partial(kernel, rows, cores), out_shape=jax.Shap...  25.7 us
    unnamed x1, local copies, waits for them, and re-layouts  0.66 us

profile of v4, /device:TPU:9, one launch (start us, length us, event | category | flops | bytes accessed | tf_op | source)
XLA Modules:
  0.0 26.4 jit_solution(13741202762972771631)
XLA Ops:
  0.0 25.7 %shard_map.37 = bf16[256,256]{1,0:T(8,128)(2,1)S(1)} custom-call(bf16[256,2,128]{2,1,0:T(2,128)(2,1)} %q_hbm.1, bf16[256,2,128]{2,1,0:T(2,128)(2,1)} %k_hbm.1, bf16[256,2,128]{2,1,0:T(2,128)(2,1)} %v_hbm.1), custom_call_target="tpu_custom_call" | custom-call | tf_op jit(solution)/shard_map/pallas_call | solution.py:180
  25.7 0.7 %copy.5 = bf16[256,256]{1,0:T(8,128)(2,1)} copy(bf16[256,256]{1,0:T(8,128)(2,1)S(1)} %shard_map.37) | data formatting | bytes 262144
